TPU v7x, 32 devices: a whole 2x2x4 slice. The times are simulated.
32 devices in a mesh: seq: 8 (over z, x), head: 4 (over y, core).
Axes of the slice: x: 2, y: 2, z: 4, core: 2. Of those that a mesh axis runs over, the one named last changes fastest.
Arguments:
- queries: bfloat16 [4096, 512], P('seq', 'head'), may hold values from -6 to 6
- key_vectors: bfloat16 [4096, 512], P('seq', 'head'), may hold values from -6 to 6
- value_vectors: bfloat16 [4096, 512], P('seq', 'head'), may hold values from -6 to 6
- attn_out: bfloat16 [4096, 512], P('seq', 'head'), may hold values from -6 to 6
- out_grad: bfloat16 [4096, 512], P('seq', 'head'), may hold values from -6 to 6
- log_norm: float32 [8, 4096], P('head', 'seq'), may hold values from 5 to 7
- doc_offsets: int32 [17], replicated, may hold values from 0 to 4096, as said below
Outputs:
- grad_queries: bfloat16 [4096, 512], P(('seq', 'head'))
- grad_keys: bfloat16 [4096, 512], P(('seq', 'head'))
- grad_values: bfloat16 [4096, 512], P(('seq', 'head'))
Inputs may be any that keep to these rules, and one draw needn't show every extreme that they name: doc_offsets[0] is 0 and doc_offsets[16] is 4096; the offsets never fall; document k holds tokens doc_offsets[k] to doc_offsets[k + 1] - 1 and may be empty; no document holds more than 1024 tokens and one holds exactly 1024.
All inputs are finite; a program needn't handle non-finite values.
Results may differ from a plain program's by a relative error of at most 0.0052.
Values may be sent and summed in bfloat16 or wider, within the bound.
A program may use at most 64 MiB of HBM per device.

v0:
```python
import functools

import jax
import jax.numpy as jnp
from jax import lax
from jax.experimental import pallas as pl
from jax.experimental.pallas import tpu as pltpu
from jax.sharding import PartitionSpec as P

MESH = pl.DeviceIdType.MESH
CHUNK = 256


def row_docs(off_ref, position):
    doc = jnp.zeros(position.shape, jnp.int32)
    for slot in range(1, off_ref.shape[0]):
        doc = doc + jnp.where(position >= off_ref[slot], 1, 0)
    return doc


def contract_last(left, right):
    return lax.dot_general(
        left, right, (((1,), (1,)), ((), ())), preferred_element_type=jnp.float32
    )


def times(left, right):
    return jnp.dot(left, right, preferred_element_type=jnp.float32)


def kernel(
    reach,
    seq_count,
    head_devs,
    heads,
    q_ref,
    k_ref,
    v_ref,
    a_ref,
    o_ref,
    n_ref,
    off_ref,
    gq_ref,
    gk_ref,
    gv_ref,
    slot_q,
    slot_o,
    slot_s,
    own_s,
    own_dq,
    part,
    back,
    dk_acc,
    dv_acc,
    k_head,
    v_head,
    k_turned,
    key_doc,
    stage,
    send_sem,
    recv_sem,
    back_send,
    back_recv,
    out_send,
    out_recv,
):
    me = lax.axis_index("seq")
    col = lax.axis_index("head")
    rows, feats = q_ref.shape
    width = feats // heads
    slots = 2 * reach
    out_rows = rows // head_devs

    def offset(i):
        return (i // 2 + 1) * (1 - 2 * (i % 2))

    def mirror(i):
        return i + 1 - 2 * (i % 2)

    def inside(i):
        other = me + offset(i)
        return (other >= 0) & (other < seq_count)

    barrier = pltpu.get_barrier_semaphore()

    count = jnp.int32(head_devs - 1)
    for i in range(slots):
        count = count + inside(i).astype(jnp.int32)

        @pl.when(inside(i))
        def _(i=i):
            pl.semaphore_signal(
                barrier, inc=1, device_id=(me + offset(i), col), device_id_type=MESH
            )

    for step in range(1, head_devs):
        pl.semaphore_signal(
            barrier,
            inc=1,
            device_id=(me, lax.rem(col + step, head_devs)),
            device_id_type=MESH,
        )
    pl.semaphore_wait(barrier, count)

    def outgoing(i, which):
        src, dst = ((q_ref, slot_q), (o_ref, slot_o), (own_s, slot_s))[which]
        return pltpu.make_async_remote_copy(
            src_ref=src,
            dst_ref=dst.at[mirror(i)],
            send_sem=send_sem.at[i, which],
            recv_sem=recv_sem.at[mirror(i), which],
            device_id=(me + offset(i), col),
            device_id_type=MESH,
        )

    def incoming(i, which):
        src, dst = ((q_ref, slot_q), (o_ref, slot_o), (own_s, slot_s))[which]
        return pltpu.make_async_remote_copy(
            src_ref=src,
            dst_ref=dst.at[i],
            send_sem=send_sem.at[i, which],
            recv_sem=recv_sem.at[i, which],
            device_id=(me + offset(i), col),
            device_id_type=MESH,
        )

    def returning(i, slot):
        return pltpu.make_async_remote_copy(
            src_ref=part.at[i],
            dst_ref=back.at[slot],
            send_sem=back_send.at[i],
            recv_sem=back_recv.at[slot],
            device_id=(me + offset(i), col),
            device_id_type=MESH,
        )

    def start_out(i, _):
        @pl.when(inside(i))
        def _():
            outgoing(i, 0).start()
            outgoing(i, 1).start()

        return 0

    lax.fori_loop(0, slots, start_out, 0)

    product = o_ref[...].astype(jnp.float32) * a_ref[...].astype(jnp.float32)
    high = product.astype(jnp.bfloat16)
    low = (product - high.astype(jnp.float32)).astype(jnp.bfloat16)
    pick_row = lax.broadcasted_iota(jnp.int32, (8, feats), 0)
    pick_col = lax.broadcasted_iota(jnp.int32, (8, feats), 1)
    pick = jnp.where(pick_row - heads == pick_col // width, 1.0, 0.0).astype(jnp.bfloat16)
    own_s[...] = contract_last(pick, high) + contract_last(pick, low)
    own_s[0:heads, :] = n_ref[...]

    def start_stats(i, _):
        @pl.when(inside(i))
        def _():
            outgoing(i, 2).start()

        return 0

    lax.fori_loop(0, slots, start_stats, 0)

    scale = width ** (-0.5)
    keys = k_ref[...].astype(jnp.float32) * scale
    values = v_ref[...].astype(jnp.float32)
    lane = lax.broadcasted_iota(jnp.int32, (rows, feats), 1)
    for h in range(heads):
        mine = (lane >= h * width) & (lane < (h + 1) * width)
        k_head[h] = jnp.where(mine, keys, 0.0).astype(jnp.bfloat16)
        v_head[h] = jnp.where(mine, values, 0.0).astype(jnp.bfloat16)
    k_turned[...] = keys.T.astype(jnp.bfloat16)
    first = me * rows
    key_doc[...] = row_docs(
        off_ref, first + lax.broadcasted_iota(jnp.int32, key_doc.shape, 0)
    )
    dk_acc[...] = jnp.zeros_like(dk_acc)
    dv_acc[...] = jnp.zeros_like(dv_acc)

    def block(q_at, o_at, s_at, base, put):
        for c in range(rows // CHUNK):
            low_t = c * CHUNK
            span = slice(low_t, low_t + CHUNK)
            query = q_at[span, :]
            grad = o_at[span, :]
            query_doc = row_docs(
                off_ref, base + low_t + lax.broadcasted_iota(jnp.int32, (1, CHUNK), 1)
            )
            docs = jnp.concatenate([key_doc[...]] * (CHUNK // key_doc.shape[1]), axis=1)
            same = docs == query_doc
            lane_c = lax.broadcasted_iota(jnp.int32, (CHUNK, feats), 1)
            dk_add, dv_add = None, None
            for h in range(heads):
                mine = (lane_c >= h * width) & (lane_c < (h + 1) * width)
                score = contract_last(k_head[h], query)
                prob = jnp.where(same, jnp.exp(score - s_at[h : h + 1, span]), 0.0)
                gp = contract_last(v_head[h], grad)
                ds = (prob * (gp - s_at[heads + h : heads + h + 1, span])).astype(
                    jnp.bfloat16
                )
                query_h = jnp.where(mine, query, jnp.bfloat16(0))
                grad_h = jnp.where(mine, grad, jnp.bfloat16(0))
                dk_h = times(ds, query_h)
                dv_h = times(prob.astype(jnp.bfloat16), grad_h)
                dk_add = dk_h if dk_add is None else dk_add + dk_h
                dv_add = dv_h if dv_add is None else dv_add + dv_h
                put(h, span, times(k_turned[h * width : (h + 1) * width, :], ds))
            dk_acc[...] += dk_add
            dv_acc[...] += dv_add

    def put_own(h, span, value):
        own_dq[h * width : (h + 1) * width, span] = value

    block(q_ref, o_ref, own_s, first, put_own)

    def visit(i, _):
        @pl.when(inside(i))
        def _():
            for which in range(3):
                incoming(i, which).wait_recv()

            def put(h, span, value):
                part[i, h * width : (h + 1) * width, span] = value.astype(jnp.bfloat16)

            block(
                slot_q.at[i],
                slot_o.at[i],
                slot_s.at[i],
                (me + offset(i)) * rows,
                put,
            )
            returning(i, mirror(i)).start()

        return 0

    lax.fori_loop(0, slots, visit, 0)

    def sharing(which, step, into):
        out = (gq_ref, gk_ref, gv_ref)[which]
        partner = lax.rem(col + step, head_devs)
        column = col if into is None else into
        return pltpu.make_async_remote_copy(
            src_ref=stage.at[which, pl.ds(pl.multiple_of(partner * out_rows, out_rows), out_rows)],
            dst_ref=out.at[:, pl.ds(pl.multiple_of(column * feats, feats), feats)],
            send_sem=out_send.at[which, step - 1],
            recv_sem=out_recv.at[which, step - 1],
            device_id=(me, partner),
            device_id_type=MESH,
        )

    def share(which):
        for step in range(1, head_devs):
            sharing(which, step, None).start()
        out = (gq_ref, gk_ref, gv_ref)[which]
        out[:, pl.ds(pl.multiple_of(col * feats, feats), feats)] = stage[
            which, pl.ds(pl.multiple_of(col * out_rows, out_rows), out_rows), :
        ]

    stage[1] = (dk_acc[...] * scale).astype(jnp.bfloat16)
    stage[2] = dv_acc[...].astype(jnp.bfloat16)
    share(1)
    share(2)

    def gather(i, _):
        @pl.when(inside(i))
        def _():
            returning(i, i).wait_recv()
            own_dq[...] += back[i].astype(jnp.float32)

        return 0

    lax.fori_loop(0, slots, gather, 0)
    stage[0] = own_dq[...].T.astype(jnp.bfloat16)
    share(0)

    def finish(i, _):
        @pl.when(inside(i))
        def _():
            for which in range(3):
                outgoing(i, which).wait_send()
            returning(i, mirror(i)).wait_send()

        return 0

    lax.fori_loop(0, slots, finish, 0)
    for which in (1, 2, 0):
        for step in range(1, head_devs):
            copy = sharing(which, step, lax.rem(col + head_devs - step, head_devs))
            copy.wait_recv()
            copy.wait_send()


def on_device(seq_count, head_devs, *args):
    queries, log_norm = args[0], args[5]
    rows, feats = queries.shape
    heads = log_norm.shape[0]
    reach = min(8, seq_count // 4)
    slots = 2 * reach
    bf16, f32 = jnp.bfloat16, jnp.float32
    vmem = pl.BlockSpec(memory_space=pltpu.VMEM)
    out = jax.ShapeDtypeStruct((rows // head_devs, feats * head_devs), bf16)
    dma = pltpu.SemaphoreType.DMA
    return pl.pallas_call(
        functools.partial(kernel, reach, seq_count, head_devs, heads),
        out_shape=(out, out, out),
        in_specs=[vmem] * 6 + [pl.BlockSpec(memory_space=pltpu.SMEM)],
        out_specs=(vmem, vmem, vmem),
        scratch_shapes=[
            pltpu.VMEM((slots, rows, feats), bf16),
            pltpu.VMEM((slots, rows, feats), bf16),
            pltpu.VMEM((slots, 8, rows), f32),
            pltpu.VMEM((8, rows), f32),
            pltpu.VMEM((feats, rows), f32),
            pltpu.VMEM((slots, feats, rows), bf16),
            pltpu.VMEM((slots, feats, rows), bf16),
            pltpu.VMEM((rows, feats), f32),
            pltpu.VMEM((rows, feats), f32),
            pltpu.VMEM((heads, rows, feats), bf16),
            pltpu.VMEM((heads, rows, feats), bf16),
            pltpu.VMEM((feats, rows), bf16),
            pltpu.VMEM((rows, 128), jnp.int32),
            pltpu.VMEM((3, rows, feats), bf16),
            dma((slots, 3)),
            dma((slots, 3)),
            dma((slots,)),
            dma((slots,)),
            dma((3, head_devs - 1)),
            dma((3, head_devs - 1)),
        ],
        compiler_params=pltpu.CompilerParams(
            collective_id=0, has_side_effects=True, vmem_limit_bytes=40 * 1024 * 1024
        ),
    )(*args)


def solution(mesh):
    seq_count, head_devs = mesh.shape["seq"], mesh.shape["head"]
    in_specs = (
        P("seq", "head"),
        P("seq", "head"),
        P("seq", "head"),
        P("seq", "head"),
        P("seq", "head"),
        P("head", "seq"),
        P(),
    )
    out_specs = (P(("seq", "head"), None),) * 3
    return jax.shard_map(
        functools.partial(on_device, seq_count, head_devs),
        mesh=mesh,
        in_specs=in_specs,
        out_specs=out_specs,
        check_vma=False,
    )
```

profile of v0, /device:TPU:0, one launch (start us, length us, event | category | flops | bytes accessed | tf_op | source)
XLA Modules:
  0.0 41.8 jit_solution(7341487862712780489)
XLA Ops:
  0.6 0.0 copy-start
  0.6 0.9 %copy-done = bf16[512,128]{1,0:T(8,128)(2,1)S(1)} copy-done((bf16[512,128]{1,0:T(8,128)(2,1)S(1)}, bf16[512,128]{1,0:T(8,128)(2,1)}, u32[]{:S(2)}) %copy-start) | copy-done | bytes 131096
  1.5 0.0 copy-start.1
  1.5 0.9 %copy-done.1 = bf16[512,128]{1,0:T(8,128)(2,1)S(1)} copy-done((bf16[512,128]{1,0:T(8,128)(2,1)S(1)}, bf16[512,128]{1,0:T(8,128)(2,1)}, u32[]{:S(2)}) %copy-start.1) | copy-done | bytes 131096
  2.4 0.0 copy-start.2
  2.4 0.9 %copy-done.2 = bf16[512,128]{1,0:T(8,128)(2,1)S(1)} copy-done((bf16[512,128]{1,0:T(8,128)(2,1)S(1)}, bf16[512,128]{1,0:T(8,128)(2,1)}, u32[]{:S(2)}) %copy-start.2) | copy-done | bytes 131096
  3.3 0.0 copy-start.3
  3.3 0.9 %copy-done.3 = bf16[512,128]{1,0:T(8,128)(2,1)S(1)} copy-done((bf16[512,128]{1,0:T(8,128)(2,1)S(1)}, bf16[512,128]{1,0:T(8,128)(2,1)}, u32[]{:S(2)}) %copy-start.3) | copy-done | bytes 131096
  4.3 0.0 copy-start.4
  4.3 0.9 %copy-done.4 = bf16[512,128]{1,0:T(8,128)(2,1)S(1)} copy-done((bf16[512,128]{1,0:T(8,128)(2,1)S(1)}, bf16[512,128]{1,0:T(8,128)(2,1)}, u32[]{:S(2)}) %copy-start.4) | copy-done | bytes 131096
  5.2 0.0 copy-start.5
  5.2 0.7 %copy-done.5 = f32[2,512]{1,0:T(2,128)S(1)} copy-done((f32[2,512]{1,0:T(2,128)S(1)}, f32[2,512]{1,0:T(2,128)}, u32[]{:S(2)}) %copy-start.5) | copy-done | bytes 4120
  5.8 0.0 copy-start.6
  5.8 0.7 %copy-done.6 = s32[17]{0:T(128)S(1)} copy-done((s32[17]{0:T(128)S(1)}, s32[17]{0:T(128)}, u32[]{:S(2)}) %copy-start.6) | copy-done | bytes 92
  6.5 33.4 %shard_map.94 = (bf16[128,512]{1,0:T(8,128)(2,1)S(1)}, bf16[128,512]{1,0:T(8,128)(2,1)S(1)}, bf16[128,512]{1,0:T(8,128)(2,1)S(1)}) custom-call(bf16[512,128]{1,0:T(8,128)(2,1)S(1)} %copy-done, bf16[512,128]{1,0:T(8,128)(2,1)S(1)} %copy-done.1, bf16[512,128]{1,0:T(8,128)(2,1)S(1)} %copy-done.2, bf16[512,128]{1,0:T(8,128)(2,1)S(1)} %copy-done.3, ...), custom_call_target="tpu_custom_call" | custom-call | tf_op jit(solution)/shard_map/pallas_call | solution.py:304
  39.9 0.7 %copy.13 = bf16[128,512]{1,0:T(8,128)(2,1)} copy(bf16[128,512]{1,0:T(8,128)(2,1)S(1)} %get-tuple-element.6) | data formatting | bytes 262144
  40.5 0.7 %copy.14 = bf16[128,512]{1,0:T(8,128)(2,1)} copy(bf16[128,512]{1,0:T(8,128)(2,1)S(1)} %get-tuple-element.7) | data formatting | bytes 262144
  41.2 0.7 %copy.15 = bf16[128,512]{1,0:T(8,128)(2,1)} copy(bf16[128,512]{1,0:T(8,128)(2,1)S(1)} %get-tuple-element.8) | data formatting | bytes 262144
Async XLA Ops:
  0.6 0.9 %copy-start = (bf16[512,128]{1,0:T(8,128)(2,1)S(1)}, bf16[512,128]{1,0:T(8,128)(2,1)}, u32[]{:S(2)}) copy-start(bf16[512,128]{1,0:T(8,128)(2,1)} %q_ref.1) | copy-start | bytes 393220
  1.5 0.9 %copy-start.1 = (bf16[512,128]{1,0:T(8,128)(2,1)S(1)}, bf16[512,128]{1,0:T(8,128)(2,1)}, u32[]{:S(2)}) copy-start(bf16[512,128]{1,0:T(8,128)(2,1)} %k_ref.1) | copy-start | bytes 393220
  2.4 0.9 %copy-start.2 = (bf16[512,128]{1,0:T(8,128)(2,1)S(1)}, bf16[512,128]{1,0:T(8,128)(2,1)}, u32[]{:S(2)}) copy-start(bf16[512,128]{1,0:T(8,128)(2,1)} %v_ref.1) | copy-start | bytes 393220
  3.3 0.9 %copy-start.3 = (bf16[512,128]{1,0:T(8,128)(2,1)S(1)}, bf16[512,128]{1,0:T(8,128)(2,1)}, u32[]{:S(2)}) copy-start(bf16[512,128]{1,0:T(8,128)(2,1)} %a_ref.1) | copy-start | bytes 393220
  4.3 0.9 %copy-start.4 = (bf16[512,128]{1,0:T(8,128)(2,1)S(1)}, bf16[512,128]{1,0:T(8,128)(2,1)}, u32[]{:S(2)}) copy-start(bf16[512,128]{1,0:T(8,128)(2,1)} %o_ref.1) | copy-start | bytes 393220
  5.2 0.7 %copy-start.5 = (f32[2,512]{1,0:T(2,128)S(1)}, f32[2,512]{1,0:T(2,128)}, u32[]{:S(2)}) copy-start(f32[2,512]{1,0:T(2,128)} %n_ref.1) | copy-start | bytes 12292
  5.8 0.7 %copy-start.6 = (s32[17]{0:T(128)S(1)}, s32[17]{0:T(128)}, u32[]{:S(2)}) copy-start(s32[17]{0:T(128)} %off_ref.1) | copy-start | bytes 208
where the time goes:
time: 42.1 us; the launch traced here: 41.8 us
  Pallas kernels  33.4 us (79%)
  local copies, waits for them, and re-layouts  7.82 us (19%)
  between operations  0.66 us (2%)
    pallas_call x1, Pallas kernels, on_device(): pl.pallas_call(functools.partial(kernel, reach, seq_count, head_devs, hea...  33.4 us
    unnamed x17, local copies, waits for them, and re-layouts  7.82 us

commit v1 on v0

--- a/solution.py
+++ b/solution.py
@@ -33,6 +33,16 @@
     seq_count,
     head_devs,
     heads,
+    q_hbm,
+    k_hbm,
+    v_hbm,
+    a_hbm,
+    o_hbm,
+    n_hbm,
+    off_hbm,
+    gq_ref,
+    gk_ref,
+    gv_ref,
     q_ref,
     k_ref,
     v_ref,
@@ -40,9 +50,7 @@
     o_ref,
     n_ref,
     off_ref,
-    gq_ref,
-    gk_ref,
-    gv_ref,
+    load_sem,
     slot_q,
     slot_o,
     slot_s,
@@ -63,6 +71,7 @@
     back_recv,
     out_send,
     out_recv,
+    keep_sem,
 ):
     me = lax.axis_index("seq")
     col = lax.axis_index("head")
@@ -81,6 +90,23 @@
         other = me + offset(i)
         return (other >= 0) & (other < seq_count)
 
+    loads = [
+        pltpu.make_async_copy(src, dst, load_sem.at[i])
+        for i, (src, dst) in enumerate(
+            (
+                (o_hbm, o_ref),
+                (a_hbm, a_ref),
+                (n_hbm, n_ref),
+                (off_hbm, off_ref),
+                (k_hbm, k_ref),
+                (v_hbm, v_ref),
+                (q_hbm, q_ref),
+            )
+        )
+    ]
+    for load in loads:
+        load.start()
+
     barrier = pltpu.get_barrier_semaphore()
 
     count = jnp.int32(head_devs - 1)
@@ -103,7 +129,7 @@
     pl.semaphore_wait(barrier, count)
 
     def outgoing(i, which):
-        src, dst = ((q_ref, slot_q), (o_ref, slot_o), (own_s, slot_s))[which]
+        src, dst = ((q_hbm, slot_q), (o_hbm, slot_o), (own_s, slot_s))[which]
         return pltpu.make_async_remote_copy(
             src_ref=src,
             dst_ref=dst.at[mirror(i)],
@@ -114,7 +140,7 @@
         )
 
     def incoming(i, which):
-        src, dst = ((q_ref, slot_q), (o_ref, slot_o), (own_s, slot_s))[which]
+        src, dst = ((q_hbm, slot_q), (o_hbm, slot_o), (own_s, slot_s))[which]
         return pltpu.make_async_remote_copy(
             src_ref=src,
             dst_ref=dst.at[i],
@@ -144,6 +170,8 @@
 
     lax.fori_loop(0, slots, start_out, 0)
 
+    for load in loads[:3]:
+        load.wait()
     product = o_ref[...].astype(jnp.float32) * a_ref[...].astype(jnp.float32)
     high = product.astype(jnp.bfloat16)
     low = (product - high.astype(jnp.float32)).astype(jnp.bfloat16)
@@ -162,6 +190,8 @@
 
     lax.fori_loop(0, slots, start_stats, 0)
 
+    for load in loads[3:]:
+        load.wait()
     scale = width ** (-0.5)
     keys = k_ref[...].astype(jnp.float32) * scale
     values = v_ref[...].astype(jnp.float32)
@@ -249,13 +279,18 @@
             device_id_type=MESH,
         )
 
+    def keeping(which):
+        out = (gq_ref, gk_ref, gv_ref)[which]
+        return pltpu.make_async_copy(
+            stage.at[which, pl.ds(pl.multiple_of(col * out_rows, out_rows), out_rows)],
+            out.at[:, pl.ds(pl.multiple_of(col * feats, feats), feats)],
+            keep_sem.at[which],
+        )
+
     def share(which):
         for step in range(1, head_devs):
             sharing(which, step, None).start()
-        out = (gq_ref, gk_ref, gv_ref)[which]
-        out[:, pl.ds(pl.multiple_of(col * feats, feats), feats)] = stage[
-            which, pl.ds(pl.multiple_of(col * out_rows, out_rows), out_rows), :
-        ]
+        keeping(which).start()
 
     stage[1] = (dk_acc[...] * scale).astype(jnp.bfloat16)
     stage[2] = dv_acc[...].astype(jnp.bfloat16)
@@ -285,6 +320,7 @@
 
     lax.fori_loop(0, slots, finish, 0)
     for which in (1, 2, 0):
+        keeping(which).wait()
         for step in range(1, head_devs):
             copy = sharing(which, step, lax.rem(col + head_devs - step, head_devs))
             copy.wait_recv()
@@ -298,15 +334,19 @@
     reach = min(8, seq_count // 4)
     slots = 2 * reach
     bf16, f32 = jnp.bfloat16, jnp.float32
-    vmem = pl.BlockSpec(memory_space=pltpu.VMEM)
+    hbm = pl.BlockSpec(memory_space=pltpu.HBM)
     out = jax.ShapeDtypeStruct((rows // head_devs, feats * head_devs), bf16)
     dma = pltpu.SemaphoreType.DMA
-    return pl.pallas_call(
+    results = pl.pallas_call(
         functools.partial(kernel, reach, seq_count, head_devs, heads),
         out_shape=(out, out, out),
-        in_specs=[vmem] * 6 + [pl.BlockSpec(memory_space=pltpu.SMEM)],
-        out_specs=(vmem, vmem, vmem),
+        in_specs=[hbm] * 7,
+        out_specs=(hbm,) * 3,
         scratch_shapes=[
+            *[pltpu.VMEM((rows, feats), bf16)] * 5,
+            pltpu.VMEM(log_norm.shape, f32),
+            pltpu.SMEM(args[6].shape, jnp.int32),
+            dma((7,)),
             pltpu.VMEM((slots, rows, feats), bf16),
             pltpu.VMEM((slots, rows, feats), bf16),
             pltpu.VMEM((slots, 8, rows), f32),
@@ -327,11 +367,29 @@
             dma((slots,)),
             dma((3, head_devs - 1)),
             dma((3, head_devs - 1)),
+            dma((3,)),
         ],
         compiler_params=pltpu.CompilerParams(
-            collective_id=0, has_side_effects=True, vmem_limit_bytes=40 * 1024 * 1024
+            collective_id=0, has_side_effects=True
         ),
     )(*args)
+    vmem = pl.BlockSpec(memory_space=pltpu.VMEM)
+    return pl.pallas_call(
+        hand_over,
+        out_shape=(out,) * 3,
+        in_specs=[vmem] * 3,
+        out_specs=(hbm,) * 3,
+        scratch_shapes=[dma((3,))],
+    )(*results)
+
+
+def hand_over(*refs):
+    sem = refs[6]
+    copies = [pltpu.make_async_copy(refs[i], refs[3 + i], sem.at[i]) for i in range(3)]
+    for copy in copies:
+        copy.start()
+    for copy in copies:
+        copy.wait()
 
 
 def solution(mesh):

time: 42.1 us -> 35.9 us (0.85)
  local copies, waits for them, and re-layouts: 7.82 us -> 0 us
  Pallas kernels: 33.4 us -> 35.1 us
    unnamed x17 -> x0, local copies, waits for them, and re-layouts: 7.82 us -> none
    pallas_call x0 -> x1, Pallas kernels: none -> 1.8 us  [on_device(): pl.pallas_call(hand_over, out_shape=(out,) * 3, in_specs=[vmem] * 3, out_...]
where the time goes in v1:
time: 35.9 us; the launch traced here: 35.7 us
  Pallas kernels  35.1 us (98%)
  between operations  0.64 us (2%)
    pallas_call x1, Pallas kernels, on_device(): pl.pallas_call(functools.partial(kernel, reach, seq_count, head_devs, hea...  33.3 us
    pallas_call x1, Pallas kernels, on_device(): pl.pallas_call(hand_over, out_shape=(out,) * 3, in_specs=[vmem] * 3, out_...  1.8 us

profile of v1, /device:TPU:0, one launch (start us, length us, event | category | flops | bytes accessed | tf_op | source)
XLA Modules:
  0.0 35.7 jit_solution(14508911710093031442)
XLA Ops:
  0.6 33.3 %shard_map.94 = (bf16[128,512]{1,0:T(8,128)(2,1)}, bf16[128,512]{1,0:T(8,128)(2,1)}, bf16[128,512]{1,0:T(8,128)(2,1)}) custom-call(bf16[512,128]{1,0:T(8,128)(2,1)} %q_hbm.1, bf16[512,128]{1,0:T(8,128)(2,1)} %k_hbm.1, bf16[512,128]{1,0:T(8,128)(2,1)} %v_hbm.1, bf16[512,128]{1,0:T(8,128)(2,1)} %a_hbm.1, bf16[512,128]{1,0:T(8,128)(2,1)} %o_hbm.1, ...), custom_call_target="tpu_custom_call" | custom-call | tf_op jit(solution)/shard_map/pallas_call | solution.py:340
  33.9 1.8 %shard_map.95 = (bf16[128,512]{1,0:T(8,128)(2,1)}, bf16[128,512]{1,0:T(8,128)(2,1)}, bf16[128,512]{1,0:T(8,128)(2,1)}) custom-call(bf16[128,512]{1,0:T(8,128)(2,1)} %get-tuple-element.6.refs_0_, bf16[128,512]{1,0:T(8,128)(2,1)} %get-tuple-element.7.refs_1_, bf16[128,512]{1,0:T(8,128)(2,1)} %get-tuple-element.8.refs_2_), custom_call_target="tpu_custom_call" | custom-call | tf_op jit(solution)/shard_map/pallas_call | solution.py:377

commit v2 on v1

--- a/solution.py
+++ b/solution.py
@@ -72,6 +72,7 @@
     out_send,
     out_recv,
     keep_sem,
+    relay_send,
 ):
     me = lax.axis_index("seq")
     col = lax.axis_index("head")
@@ -160,6 +161,46 @@
             device_id_type=MESH,
         )
 
+    odd = lax.rem(me, 2)
+    direct, diagonal = odd, 1 - odd
+    ahead, behind = 2 + odd, 3 - odd
+
+    def when_inside(i, act):
+        @pl.when(inside(i))
+        def _():
+            act()
+
+    def relay_q():
+        return pltpu.make_async_remote_copy(
+            src_ref=slot_q.at[direct],
+            dst_ref=slot_q.at[diagonal],
+            send_sem=relay_send.at[0],
+            recv_sem=recv_sem.at[diagonal, 0],
+            device_id=(me + offset(ahead), col),
+            device_id_type=MESH,
+        )
+
+    def relay_o():
+        return pltpu.make_async_remote_copy(
+            src_ref=slot_o.at[ahead],
+            dst_ref=slot_o.at[odd],
+            send_sem=relay_send.at[1],
+            recv_sem=recv_sem.at[odd, 1],
+            device_id=(me + offset(direct), col),
+            device_id_type=MESH,
+        )
+
+    outgoing(direct, 0).start()
+    when_inside(behind, lambda: outgoing(behind, 1).start())
+    outgoing(direct, 1).start()
+    when_inside(behind, lambda: outgoing(behind, 0).start())
+
+    def send_ahead():
+        outgoing(ahead, 0).start()
+        outgoing(ahead, 1).start()
+
+    when_inside(ahead, send_ahead)
+
     def start_out(i, _):
         @pl.when(inside(i))
         def _():
@@ -168,7 +209,7 @@
 
         return 0
 
-    lax.fori_loop(0, slots, start_out, 0)
+    lax.fori_loop(4, slots, start_out, 0)
 
     for load in loads[:3]:
         load.wait()
@@ -244,27 +285,33 @@
 
     block(q_ref, o_ref, own_s, first, put_own)
 
-    def visit(i, _):
-        @pl.when(inside(i))
-        def _():
-            for which in range(3):
-                incoming(i, which).wait_recv()
-
-            def put(h, span, value):
-                part[i, h * width : (h + 1) * width, span] = value.astype(jnp.bfloat16)
-
-            block(
-                slot_q.at[i],
-                slot_o.at[i],
-                slot_s.at[i],
-                (me + offset(i)) * rows,
-                put,
-            )
-            returning(i, mirror(i)).start()
-
+    def relay():
+        incoming(ahead, 1).wait_recv()
+        relay_o().start()
+
+    incoming(direct, 0).wait_recv()
+    when_inside(ahead, lambda: relay_q().start())
+    when_inside(ahead, relay)
+
+    def visit(i, waits):
+        for which in waits:
+            incoming(i, which).wait_recv()
+
+        def put(h, span, value):
+            part[i, h * width : (h + 1) * width, span] = value.astype(jnp.bfloat16)
+
+        block(slot_q.at[i], slot_o.at[i], slot_s.at[i], (me + offset(i)) * rows, put)
+        returning(i, mirror(i)).start()
+
+    def visit_rest(i, _):
+        when_inside(i, lambda: visit(i, (0, 1, 2)))
         return 0
 
-    lax.fori_loop(0, slots, visit, 0)
+    visit(direct, (1, 2))
+    when_inside(ahead, lambda: visit(ahead, (0, 2)))
+    when_inside(behind, lambda: visit(behind, (0, 1, 2)))
+    when_inside(diagonal, lambda: visit(diagonal, (0, 1, 2)))
+    lax.fori_loop(4, slots, visit_rest, 0)
 
     def sharing(which, step, into):
         out = (gq_ref, gk_ref, gv_ref)[which]
@@ -318,7 +365,18 @@
 
         return 0
 
-    lax.fori_loop(0, slots, finish, 0)
+    def finish_diagonal():
+        outgoing(diagonal, 2).wait_send()
+        returning(diagonal, mirror(diagonal)).wait_send()
+
+    def finish_relay():
+        relay_q().wait_send()
+        relay_o().wait_send()
+
+    finish(direct, 0)
+    when_inside(diagonal, finish_diagonal)
+    when_inside(ahead, finish_relay)
+    lax.fori_loop(2, slots, finish, 0)
     for which in (1, 2, 0):
         keeping(which).wait()
         for step in range(1, head_devs):
@@ -368,6 +426,7 @@
             dma((3, head_devs - 1)),
             dma((3, head_devs - 1)),
             dma((3,)),
+            dma((2,)),
         ],
         compiler_params=pltpu.CompilerParams(
             collective_id=0, has_side_effects=True

time: 35.9 us -> 29.9 us (0.83)
  the two profiles are of different devices: /device:TPU:0 before, /device:TPU:11 now
where the time goes in v2:
time: 29.9 us; the launch traced here: 29.8 us
  Pallas kernels  29.1 us (97%)
  between operations  0.64 us (2%)
    pallas_call x1, Pallas kernels, on_device(): pl.pallas_call(functools.partial(kernel, reach, seq_count, head_devs, hea...  27.3 us
    pallas_call x1, Pallas kernels, on_device(): pl.pallas_call(hand_over, out_shape=(out,) * 3, in_specs=[vmem] * 3, out_...  1.8 us

profile of v2, /device:TPU:11, one launch (start us, length us, event | category | flops | bytes accessed | tf_op | source)
XLA Modules:
  0.0 29.8 jit_solution(5216032255141079530)
XLA Ops:
  0.6 27.3 %shard_map.94 = (bf16[128,512]{1,0:T(8,128)(2,1)}, bf16[128,512]{1,0:T(8,128)(2,1)}, bf16[128,512]{1,0:T(8,128)(2,1)}) custom-call(bf16[512,128]{1,0:T(8,128)(2,1)} %q_hbm.1, bf16[512,128]{1,0:T(8,128)(2,1)} %k_hbm.1, bf16[512,128]{1,0:T(8,128)(2,1)} %v_hbm.1, bf16[512,128]{1,0:T(8,128)(2,1)} %a_hbm.1, bf16[512,128]{1,0:T(8,128)(2,1)} %o_hbm.1, ...), custom_call_target="tpu_custom_call" | custom-call | tf_op jit(solution)/shard_map/pallas_call | solution.py:398
  28.0 1.8 %shard_map.95 = (bf16[128,512]{1,0:T(8,128)(2,1)}, bf16[128,512]{1,0:T(8,128)(2,1)}, bf16[128,512]{1,0:T(8,128)(2,1)}) custom-call(bf16[128,512]{1,0:T(8,128)(2,1)} %get-tuple-element.6.refs_0_, bf16[128,512]{1,0:T(8,128)(2,1)} %get-tuple-element.7.refs_1_, bf16[128,512]{1,0:T(8,128)(2,1)} %get-tuple-element.8.refs_2_), custom_call_target="tpu_custom_call" | custom-call | tf_op jit(solution)/shard_map/pallas_call | solution.py:436

commit v3 on v2

--- a/solution.py
+++ b/solution.py
@@ -309,8 +309,8 @@
 
     visit(direct, (1, 2))
     when_inside(ahead, lambda: visit(ahead, (0, 2)))
+    when_inside(diagonal, lambda: visit(diagonal, (0, 1, 2)))
     when_inside(behind, lambda: visit(behind, (0, 1, 2)))
-    when_inside(diagonal, lambda: visit(diagonal, (0, 1, 2)))
     lax.fori_loop(4, slots, visit_rest, 0)
 
     def sharing(which, step, into):

time: 29.9 us -> 31 us (1.037)
  the two profiles are of different devices: /device:TPU:11 before, /device:TPU:0 now
where the time goes in v3:
time: 31 us; the launch traced here: 30.8 us
  Pallas kernels  30.2 us (97%)
  between operations  0.64 us (2%)
    pallas_call x1, Pallas kernels, on_device(): pl.pallas_call(functools.partial(kernel, reach, seq_count, head_devs, hea...  28.4 us
    pallas_call x1, Pallas kernels, on_device(): pl.pallas_call(hand_over, out_shape=(out,) * 3, in_specs=[vmem] * 3, out_...  1.8 us

profile of v3, /device:TPU:0, one launch (start us, length us, event | category | flops | bytes accessed | tf_op | source)
XLA Modules:
  0.0 30.8 jit_solution(12950851744196695457)
XLA Ops:
  0.6 28.4 %shard_map.94 = (bf16[128,512]{1,0:T(8,128)(2,1)}, bf16[128,512]{1,0:T(8,128)(2,1)}, bf16[128,512]{1,0:T(8,128)(2,1)}) custom-call(bf16[512,128]{1,0:T(8,128)(2,1)} %q_hbm.1, bf16[512,128]{1,0:T(8,128)(2,1)} %k_hbm.1, bf16[512,128]{1,0:T(8,128)(2,1)} %v_hbm.1, bf16[512,128]{1,0:T(8,128)(2,1)} %a_hbm.1, bf16[512,128]{1,0:T(8,128)(2,1)} %o_hbm.1, ...), custom_call_target="tpu_custom_call" | custom-call | tf_op jit(solution)/shard_map/pallas_call | solution.py:398
  29.0 1.8 %shard_map.95 = (bf16[128,512]{1,0:T(8,128)(2,1)}, bf16[128,512]{1,0:T(8,128)(2,1)}, bf16[128,512]{1,0:T(8,128)(2,1)}) custom-call(bf16[128,512]{1,0:T(8,128)(2,1)} %get-tuple-element.6.refs_0_, bf16[128,512]{1,0:T(8,128)(2,1)} %get-tuple-element.7.refs_1_, bf16[128,512]{1,0:T(8,128)(2,1)} %get-tuple-element.8.refs_2_), custom_call_target="tpu_custom_call" | custom-call | tf_op jit(solution)/shard_map/pallas_call | solution.py:436
